TPU v7x, 32 devices: a whole 2x2x4 slice. The times are simulated.
32 devices in a mesh: member: 4 (over z), dp: 8 (over y, x, core).
Axes of the slice: x: 2, y: 2, z: 4, core: 2. Of those that a mesh axis runs over, the one named last changes fastest.
Arguments:
- latents: bfloat16 [4, 32, 16, 16, 640], P('member', 'dp'), may hold values from -6 to 6
- cotangent: bfloat16 [4, 32, 16, 16, 640], P('member', 'dp'), may hold values from -6 to 6
- weights: float32 [4, 640, 5760], P('member', 'dp'), may hold values from -6 to 6
- first_moment: float32 [4, 640, 5760], P('member', 'dp'), may hold values from -1.2 to 1.2
- second_moment: float32 [4, 640, 5760], P('member', 'dp'), may hold values from 0.02 to 0.5
- sources: int32 [4], replicated, may hold values from 0 to 3, as said below
Outputs:
- latent_grad: bfloat16 [4, 32, 16, 16, 640], P('member', 'dp')
- new_weights: float32 [4, 640, 5760], P('member', 'dp')
- new_first: float32 [4, 640, 5760], P('member', 'dp')
- new_second: float32 [4, 640, 5760], P('member', 'dp')
Inputs may be any that keep to these rules, and one draw needn't show every extreme that they name: sources[k] = k for every member that takes no copy; a member that takes a copy names a member that names itself; at most one quarter of the members (at least one) take copies, and at most one quarter (at least one) are named by others.
All inputs are finite; a program needn't handle non-finite values.
Results may differ from a plain program's by a relative error of at most 0.006.
Values may be sent and summed in bfloat16 or wider, within the bound.
A program may use at most 128 MiB of HBM per device.

v0:
```python
import jax
import jax.numpy as jnp
from jax import lax
from jax.experimental import pallas as pl
from jax.experimental.pallas import tpu as pltpu
from jax.sharding import PartitionSpec as P

CH_IN = 640
ADAM_STEP = 10


BETA_ONE = 0.9
BETA_TWO = 0.99
RATE = 0.05
EPSILON = 1e-08


def silu_slope(values):
    sig = jax.nn.sigmoid(values)
    return sig * (1.0 + values * (1.0 - sig))


def forward_taps(activation, kernel_bf):
    side_cells = activation.shape[1]
    cell_count = activation.shape[0] * side_cells * side_cells
    cols_out = kernel_bf.shape[1] // 9
    padded = jnp.pad(activation, ((0, 0), (1, 1), (1, 1), (0, 0)))
    summed = jnp.zeros((cell_count, cols_out), jnp.float32)
    for tap_index in range(9):
        tap_row = tap_index // 3
        tap_col = tap_index % 3
        window = padded[
            :, tap_row : tap_row + side_cells, tap_col : tap_col + side_cells, :
        ].reshape(cell_count, activation.shape[3])
        summed = summed + jnp.dot(
            window,
            kernel_bf[:, tap_index * cols_out : (tap_index + 1) * cols_out],
            preferred_element_type=jnp.float32,
        )
    return summed


def backward_taps(deltas, kernel_bf):
    side_cells = deltas.shape[1]
    cell_count = deltas.shape[0] * side_cells * side_cells
    cols_out = deltas.shape[3]
    padded = jnp.pad(deltas, ((0, 0), (1, 1), (1, 1), (0, 0)))
    summed = jnp.zeros((cell_count, kernel_bf.shape[0]), jnp.float32)
    for tap_index in range(9):
        tap_row = tap_index // 3
        tap_col = tap_index % 3
        window = padded[
            :, 2 - tap_row : 2 - tap_row + side_cells, 2 - tap_col : 2 - tap_col + side_cells, :
        ].reshape(cell_count, cols_out)
        block = kernel_bf[:, tap_index * cols_out : (tap_index + 1) * cols_out]
        summed = summed + lax.dot_general(
            window, block, (((1,), (1,)), ((), ())), preferred_element_type=jnp.float32
        )
    return summed


def weight_taps(activation, deltas):
    side_cells = activation.shape[1]
    cell_count = activation.shape[0] * side_cells * side_cells
    flat_deltas = deltas.reshape(cell_count, deltas.shape[3])
    padded = jnp.pad(activation, ((0, 0), (1, 1), (1, 1), (0, 0)))
    blocks = []
    for tap_index in range(9):
        tap_row = tap_index // 3
        tap_col = tap_index % 3
        window = padded[
            :, tap_row : tap_row + side_cells, tap_col : tap_col + side_cells, :
        ].reshape(cell_count, activation.shape[3])
        blocks.append(
            lax.dot_general(
                window, flat_deltas, (((0,), (0,)), ((), ())), preferred_element_type=jnp.float32
            )
        )
    return jnp.concatenate(blocks, axis=1)


def adam_update(weights_now, first_now, second_now, gradient):
    first_new = BETA_ONE * first_now + (1.0 - BETA_ONE) * gradient
    second_new = BETA_TWO * second_now + (1.0 - BETA_TWO) * gradient * gradient
    first_fix = 1.0 - BETA_ONE**ADAM_STEP
    second_fix = 1.0 - BETA_TWO**ADAM_STEP
    updated = weights_now - RATE * (first_new / first_fix) / (
        jnp.sqrt(second_new / second_fix) + EPSILON
    )
    return (updated, first_new, second_new)


def takers_and_named(sources):
    members = sources.shape[0]
    slots = max(members // 4, 1)
    own = jnp.arange(members, dtype=jnp.int32)
    takers = jnp.argsort(jnp.where(sources == own, 1, 0), stable=True)[:slots]
    return takers, sources[takers]


def carry_over(stacked, takers, named):
    me = lax.axis_index("member")
    sent = [
        jnp.where(named[slot] == me, stacked, jnp.zeros_like(stacked))
        for slot in range(takers.shape[0])
    ]
    arrived = lax.psum(jnp.stack(sent), "member")
    return arrived


def local_plain(latents, cotangent, weights, first_moment, second_moment, sources):
    scale = (9 * CH_IN) ** (-0.5)
    me = lax.axis_index("member")
    takers, named = takers_and_named(sources)
    images = latents[0]
    activation = jax.nn.silu(images.astype(jnp.float32)).astype(jnp.bfloat16)
    kernel_rows = weights[0].astype(jnp.bfloat16)
    state = jnp.concatenate(
        [kernel_rows, first_moment[0].astype(jnp.bfloat16), second_moment[0].astype(jnp.bfloat16)]
    )
    cell_count = images.shape[0] * images.shape[1] * images.shape[2]
    cols_out = cotangent.shape[4]
    kernel_all = lax.all_gather(kernel_rows, "dp", axis=0, tiled=True)
    arrived = carry_over(state, takers, named)
    hidden = scale * forward_taps(activation, kernel_all)
    deltas = (
        cotangent[0].reshape(cell_count, cols_out).astype(jnp.float32) * silu_slope(hidden)
    ).astype(jnp.bfloat16)
    deltas_img = deltas.reshape(cotangent[0].shape)
    back = scale * backward_taps(deltas_img, kernel_all)
    slope_in = silu_slope(images.reshape(cell_count, images.shape[3]).astype(jnp.float32))
    latent_grad = (back * slope_in).astype(jnp.bfloat16).reshape(latents.shape)
    gradient = lax.psum_scatter(
        (scale * weight_taps(activation, deltas_img)).astype(jnp.bfloat16),
        "dp",
        scatter_dimension=0,
        tiled=True,
    )
    gradient, arrived = lax.optimization_barrier((gradient, arrived))
    moved_gradient = carry_over(gradient, takers, named)
    rows = gradient.shape[0]
    weights_now, first_now, second_now = weights[0], first_moment[0], second_moment[0]
    gradient = gradient.astype(jnp.float32)
    for slot in range(takers.shape[0]):
        taking = (takers[slot] == me) & (named[slot] != me)
        moved = arrived[slot].astype(jnp.float32)
        weights_now = jnp.where(taking, moved[:rows], weights_now)
        first_now = jnp.where(taking, moved[rows : 2 * rows], first_now)
        second_now = jnp.where(taking, moved[2 * rows :], second_now)
        gradient = jnp.where(taking, moved_gradient[slot].astype(jnp.float32), gradient)
    updated, first_new, second_new = adam_update(weights_now, first_now, second_now, gradient)
    return (latent_grad, updated[None], first_new[None], second_new[None])


HALF = 48


def shifted(values):
    none = jnp.zeros((1, values.shape[1]), jnp.float32)
    before = jnp.concatenate([none, values[:-1]], axis=0)
    after = jnp.concatenate([values[1:], none], axis=0)
    return before, values, after


def block_kernel(
    flags,
    latents,
    cotangent,
    state,
    latent_grad,
    grad,
    arrived,
    moved,
    kall,
    near,
    act_t,
    total,
    partial,
    core_in,
    chip_sum,
    x_in,
    y_in,
    a_sum,
    b_sum,
    a_in,
    b_in,
    up_in,
    down_in,
    up_grad,
    down_grad,
    ag_send,
    ag_recv,
    rs_send,
    rs_recv,
    z_send,
    z_recv,
):
    images, side = latents.shape[0], latents.shape[1]
    width = latents.shape[3]
    cells = side * side
    rows = state.shape[2]
    scale = (9 * CH_IN) ** (-0.5)
    f32, bf16 = jnp.float32, jnp.bfloat16
    k = lax.axis_index("member")
    me = lax.axis_index("dp")
    y, x, c = me // 4, (me // 2) % 2, me % 2
    sib = me + 1 - 2 * c
    xp = me + 2 - 4 * x
    yp = me + 4 - 8 * y
    diag = xp + 4 - 8 * y
    named = flags[0]
    from_below = flags[1]

    def remote(src, dst, send, recv, member, index):
        return pltpu.make_async_remote_copy(
            src_ref=src,
            dst_ref=dst,
            send_sem=send,
            recv_sem=recv,
            device_id=(member, index),
            device_id_type=pl.DeviceIdType.MESH,
        )

    barrier = pltpu.get_barrier_semaphore()
    for peer in (sib, xp, yp):
        pl.semaphore_signal(
            barrier, inc=1, device_id=(k, peer), device_id_type=pl.DeviceIdType.MESH
        )

    @pl.when(k < 3)
    def _():
        pl.semaphore_signal(
            barrier, inc=1, device_id=(k + 1, me), device_id_type=pl.DeviceIdType.MESH
        )

    @pl.when(k > 0)
    def _():
        pl.semaphore_signal(
            barrier, inc=1, device_id=(k - 1, me), device_id_type=pl.DeviceIdType.MESH
        )

    pl.semaphore_wait(barrier, 3 + jnp.where(k < 3, 1, 0) + jnp.where(k > 0, 1, 0))

    def block(t, owner, first=0, count=rows):
        return kall.at[t, owner, pl.ds(first, count)]

    def gather(t, kind):
        if kind < 3:
            part, peer = block(t, me), (sib, xp, yp)[kind]
        elif kind == 3:
            part, peer = block(t, xp, 0, HALF), yp
        elif kind == 4:
            part, peer = block(t, yp, HALF, rows - HALF), xp
        else:
            part, peer = block(t, (xp, yp, diag)[kind - 5]), sib
        return remote(part, part, ag_send.at[t, kind], ag_recv.at[t, kind], k, peer)

    def gather_wait(t, kind):
        gather_in(t, kind).wait_recv()

    def gather_in(t, kind):
        if kind < 3:
            part = block(t, (sib, xp, yp)[kind])
        elif kind == 3:
            part = block(t, diag, 0, HALF)
        elif kind == 4:
            part = block(t, diag, HALF, rows - HALF)
        else:
            over = 1 - 2 * c
            part = block(t, (xp + over, yp + over, diag + over)[kind - 5])
        return remote(part, part, ag_send.at[t, kind], ag_recv.at[t, kind], k, sib)

    def state_step(tick, lane, rank, here, target):
        j = tick // 2 - 2 * rank

        @pl.when((tick % 2 == 0) & (j >= 0) & (j < 9) & (rank < 3))
        def _():
            @pl.when(rank == 0)
            def _():
                here[j] = state[j]

            @pl.when(rank > 0)
            def _():
                remote(
                    here.at[j], here.at[j], z_send.at[lane, j], z_recv.at[lane, j], target, me
                ).wait_recv()
                mine, came = state[j].astype(f32), here[j].astype(f32)
                here[j] = (mine * named + came * (1.0 - named)).astype(bf16)

            remote(
                here.at[j], here.at[j], z_send.at[lane, j], z_recv.at[lane, j], target, me
            ).start()

    def grad_step(tick, lane, rank, here, target):
        t = tick - 14 - 2 * rank

        @pl.when((t >= 0) & (t < 9) & (rank < 3))
        def _():
            copy = remote(
                here.at[t], here.at[t], z_send.at[lane, t], z_recv.at[lane, t], target, me
            )

            @pl.when(rank == 0)
            def _():
                here[t] = grad[t]

            @pl.when(rank > 0)
            def _():
                copy.wait_recv()
                mine, came = grad[t].astype(f32), here[t].astype(f32)
                here[t] = (mine * named + came * (1.0 - named)).astype(bf16)

            copy.start()

    def member_steps(tick, with_grad):
        state_step(tick, 0, k, up_in, jnp.minimum(k + 1, 3))
        state_step(tick, 1, 3 - k, down_in, jnp.maximum(k - 1, 0))
        if with_grad:
            grad_step(tick, 2, k, up_grad, jnp.minimum(k + 1, 3))
            grad_step(tick, 3, 3 - k, down_grad, jnp.maximum(k - 1, 0))

    def cast_tap(t, carry):
        kall[t, me] = state[t, 0]
        return carry

    lax.fori_loop(0, 9, cast_tap, 0)

    def first_sends(t):
        for kind in range(3):
            gather(t, kind).start()

    def ahead(t, carry):
        first_sends(t)
        return carry

    lax.fori_loop(0, 4, ahead, 0)

    zero_row = jnp.zeros((side, width), bf16)

    def clear(n, carry):
        near[n // images, n % images, 0] = zero_row
        near[n // images, n % images, side + 1] = zero_row
        return carry

    lax.fori_loop(0, 3 * images, clear, 0)

    def activate(n, carry):
        b, i = n // side, n % side
        value = latents[b, i].astype(f32)
        value = value / (1.0 + jnp.exp(-value))
        for at, moved_values in enumerate(shifted(value)):
            near[at, b, i + 1] = moved_values.astype(bf16)
        return carry

    lax.fori_loop(0, images * side, activate, 0)
    for b in range(images):
        flat = near[1, b, 1 : side + 1].reshape(cells, width)
        act_t[:, b * cells : (b + 1) * cells] = jnp.transpose(flat)

    def forward(i, carry):
        @pl.when(i < 9)
        def _():
            member_steps(i, False)

        @pl.when(i + 4 < 9)
        def _():
            first_sends(i + 4)

        @pl.when(i < 9)
        def _():
            gather_wait(i, 1)
            gather_wait(i, 2)
            for kind in (3, 4, 5, 6):
                gather(i, kind).start()

        @pl.when((i >= 1) & (i < 10))
        def _():
            gather_wait(i - 1, 3)
            gather_wait(i - 1, 4)
            gather(i - 1, 7).start()

        @pl.when(i >= 2)
        def _():
            t = i - 2
            for kind in (0, 5, 6, 7):
                gather_wait(t, kind)
            weight = kall[t].reshape(8 * rows, width)

            def one(b, carry):
                window = near[t % 3, b, pl.ds(t // 3, side)].reshape(cells, width)
                product = jnp.dot(window, weight, preferred_element_type=f32)
                total[b] = jnp.where(t == 0, 0.0, total[b]) + product
                return carry

            lax.fori_loop(0, images, one, 0)

        return carry

    lax.fori_loop(0, 11, forward, 0)

    def slope_rows(n, carry):
        b, i = n // side, n % side
        hidden = scale * total[b, pl.ds(pl.multiple_of(i * side, side), side)]
        value = cotangent[b, i].astype(f32) * silu_slope(hidden)
        for at, moved_values in enumerate(shifted(value)):
            near[at, b, i + 1] = moved_values.astype(bf16)
        return carry

    lax.fori_loop(0, images * side, slope_rows, 0)

    def window_of(t, b):
        return near[2 - t % 3, b, pl.ds(2 - t // 3, side)].reshape(cells, width)

    def scatter(t, kind):
        if kind == 0:
            src, dst, peer = partial.at[t, :, :, 1 - c], core_in.at[t], sib
        elif kind == 1:
            src, dst, peer = chip_sum.at[t, :, 1 - x, pl.ds(0, HALF)], x_in.at[t], xp
        elif kind == 2:
            src, dst, peer = chip_sum.at[t, 1 - y, :, pl.ds(HALF, rows - HALF)], y_in.at[t], yp
        elif kind == 3:
            src, dst, peer = a_sum.at[t, 1 - y], a_in.at[t], yp
        else:
            src, dst, peer = b_sum.at[t, 1 - x], b_in.at[t], xp
        return remote(src, dst, rs_send.at[t, kind], rs_recv.at[t, kind], k, peer)

    def plus(one, two):
        return (one.astype(f32) + two.astype(f32)).astype(bf16)

    def scatter_steps(i):
        @pl.when((i >= 1) & (i < 10))
        def _():
            t = i - 1
            scatter(t, 0).wait_recv()
            for yy in range(2):
                for xx in range(2):
                    chip_sum[t, yy, xx] = plus(partial[t, yy, xx, c], core_in[t, yy, xx])
            scatter(t, 1).start()
            scatter(t, 2).start()

        @pl.when((i >= 3) & (i < 12))
        def _():
            t = i - 3
            scatter(t, 1).wait_recv()
            scatter(t, 2).wait_recv()
            for at in range(2):
                a_sum[t, at] = plus(chip_sum[t, at, x, 0:HALF], x_in[t, at])
                b_sum[t, at] = plus(chip_sum[t, y, at, HALF:rows], y_in[t, at])
            scatter(t, 3).start()
            scatter(t, 4).start()

        @pl.when((i >= 5) & (i < 14))
        def _():
            t = i - 5
            scatter(t, 3).wait_recv()
            scatter(t, 4).wait_recv()
            grad[t, 0:HALF] = plus(a_sum[t, y], a_in[t])
            grad[t, HALF:rows] = plus(b_sum[t, x], b_in[t])

    def kernel_grad(t, carry):
        scatter_steps(t)
        member_steps(t + 9, True)
        window = near[2 - t % 3, :, pl.ds(2 - t // 3, side)].reshape(images * cells, width)

        def one(yy, carry):
            lhs = act_t[pl.ds(pl.multiple_of(yy * 4 * rows, 64), 4 * rows)]
            product = scale * jnp.dot(lhs, window, preferred_element_type=f32)
            partial[t, yy] = product.astype(bf16).reshape(2, 2, rows, width)
            return carry

        lax.fori_loop(0, 2, one, 0)
        scatter(t, 0).start()
        return carry

    lax.fori_loop(0, 9, kernel_grad, 0)

    def back(t, carry):
        scatter_steps(t + 9)
        member_steps(t + 18, True)
        weight = kall[t].reshape(8 * rows, width)

        def one(b, carry):
            product = lax.dot_general(
                window_of(t, b), weight, (((1,), (1,)), ((), ())), preferred_element_type=f32
            )
            total[b] = jnp.where(t == 0, 0.0, total[b]) + product
            return carry

        lax.fori_loop(0, images, one, 0)
        return carry

    lax.fori_loop(0, 9, back, 0)

    def finish(n, carry):
        b, i = n // side, n % side
        value = scale * total[b, pl.ds(pl.multiple_of(i * side, side), side)]
        value = value * silu_slope(latents[b, i].astype(f32))
        latent_grad[b, i] = value.astype(bf16)
        return carry

    lax.fori_loop(0, images * side, finish, 0)

    def pick(dst, below, above, j):
        @pl.when(k == 0)
        def _():
            dst[j] = above[j]

        @pl.when(k == 3)
        def _():
            dst[j] = below[j]

        @pl.when((k > 0) & (k < 3))
        def _():
            lower, upper = below[j].astype(f32), above[j].astype(f32)
            dst[j] = (lower * from_below + upper * (1.0 - from_below)).astype(bf16)

    def drain(j, carry):
        for lane, here in enumerate((up_in, down_in, up_grad, down_grad)):
            copy = remote(here.at[j], here.at[j], z_send.at[lane, j], z_recv.at[lane, j], k, sib)
            last = k == 3 if lane % 2 == 0 else k == 0

            @pl.when(last)
            def _():
                copy.wait_recv()

            @pl.when(jnp.logical_not(last))
            def _():
                copy.wait_send()

        pick(arrived, up_in, down_in, j)
        pick(moved, up_grad, down_grad, j)
        for kind in range(8):
            gather(j, kind).wait_send()
        for kind in range(5):
            scatter(j, kind).wait_send()
        return carry

    lax.fori_loop(0, 9, drain, 0)


def local_block(latents, cotangent, weights, first_moment, second_moment, sources):
    me = lax.axis_index("member")
    takers, named = takers_and_named(sources)
    taker, source = takers[0], named[0]
    rows, width = weights.shape[1], latents.shape[4]
    bf16 = jnp.bfloat16
    state = jnp.stack([weights[0], first_moment[0], second_moment[0]]).astype(bf16)
    state = state.reshape(3, rows, 9, width).transpose(2, 0, 1, 3)
    flags = jnp.stack([source == me, source < taker]).astype(jnp.float32)
    images, side = latents.shape[1], latents.shape[2]
    cells = side * side
    vmem = pl.BlockSpec(memory_space=pltpu.VMEM)
    tap = (9, rows, width)
    half, rest = HALF, rows - HALF
    latent_grad, grad, arrived, moved = pl.pallas_call(
        block_kernel,
        out_shape=(
            jax.ShapeDtypeStruct(latents.shape[1:], bf16),
            jax.ShapeDtypeStruct(tap, bf16),
            jax.ShapeDtypeStruct((9, 3, rows, width), bf16),
            jax.ShapeDtypeStruct(tap, bf16),
        ),
        in_specs=[pl.BlockSpec(memory_space=pltpu.SMEM), vmem, vmem, vmem],
        out_specs=(vmem,) * 4,
        scratch_shapes=[
            pltpu.VMEM((9, 8, rows, width), bf16),
            pltpu.VMEM((3, images, side + 2, side, width), bf16),
            pltpu.VMEM((width, images * cells), bf16),
            pltpu.VMEM((images, cells, width), jnp.float32),
            pltpu.VMEM((9, 2, 2, 2, rows, width), bf16),
            pltpu.VMEM((9, 2, 2, rows, width), bf16),
            pltpu.VMEM((9, 2, 2, rows, width), bf16),
            pltpu.VMEM((9, 2, half, width), bf16),
            pltpu.VMEM((9, 2, rest, width), bf16),
            pltpu.VMEM((9, 2, half, width), bf16),
            pltpu.VMEM((9, 2, rest, width), bf16),
            pltpu.VMEM((9, half, width), bf16),
            pltpu.VMEM((9, rest, width), bf16),
            pltpu.VMEM((9, 3, rows, width), bf16),
            pltpu.VMEM((9, 3, rows, width), bf16),
            pltpu.VMEM(tap, bf16),
            pltpu.VMEM(tap, bf16),
            pltpu.SemaphoreType.DMA((9, 8)),
            pltpu.SemaphoreType.DMA((9, 8)),
            pltpu.SemaphoreType.DMA((9, 5)),
            pltpu.SemaphoreType.DMA((9, 5)),
            pltpu.SemaphoreType.DMA((4, 9)),
            pltpu.SemaphoreType.DMA((4, 9)),
        ],
        compiler_params=pltpu.CompilerParams(
            collective_id=0, has_side_effects=True, vmem_limit_bytes=60 * 1024 * 1024
        ),
        cost_estimate=pl.CostEstimate(
            flops=6 * images * cells * 9 * width * width, bytes_accessed=16000000, transcendentals=0
        ),
    )(flags, latents[0], cotangent[0], state)

    def flat(taps):
        return taps.astype(jnp.float32).transpose(1, 0, 2).reshape(rows, 9 * width)

    taking = (taker == me) & (source != me)
    weights_now = jnp.where(taking, flat(arrived[:, 0]), weights[0])
    first_now = jnp.where(taking, flat(arrived[:, 1]), first_moment[0])
    second_now = jnp.where(taking, flat(arrived[:, 2]), second_moment[0])
    gradient = flat(jnp.where(taking, moved, grad))
    updated, first_new, second_new = adam_update(weights_now, first_now, second_now, gradient)
    return (latent_grad[None], updated[None], first_new[None], second_new[None])


def solution(mesh):
    fits = mesh.shape["member"] == 4 and mesh.shape["dp"] == 8
    local = local_block if fits else local_plain
    in_specs = (
        P("member", "dp", None, None, None),
        P("member", "dp", None, None, None),
        P("member", "dp", None),
        P("member", "dp", None),
        P("member", "dp", None),
        P(),
    )
    out_specs = (
        P("member", "dp", None, None, None),
        P("member", "dp", None),
        P("member", "dp", None),
        P("member", "dp", None),
    )
    return jax.shard_map(local, mesh=mesh, in_specs=in_specs, out_specs=out_specs, check_vma=False)
```

profile of v0, /device:TPU:0, one launch (start us, length us, event | category | flops | bytes accessed | tf_op | source)
XLA Modules:
  0.0 174.8 jit_solution(2044109151014335058)
XLA Ops:
  0.6 0.7 compare_select_fusion
  1.3 0.7 sort.17
  2.2 1.2 dynamic-slice.2
  5.4 0.6 add_convert_fusion.flags
  6.0 0.0 copy-start.1
  6.0 1.7 convert.23
  7.7 0.1 copy.23
  7.8 0.0 copy-start
  7.8 0.2 copy-done.1
  8.0 0.1 convert.24
  8.1 1.2 copy-done
  9.4 0.1 convert.25
  9.5 0.3 copy_bitcast_fusion
  9.7 1.9 %maximum_bitcast_fusion.state = bf16[9,3,80,640]{3,2,1,0:T(8,128)(2,1)} fusion(bf16[1,80,9,640]{3,1,0,2:T(8,128)(2,1)S(1)} %get-tuple-element.31, bf16[1,80,9,640]{3,1,0,2:T(8,128)(2,1)S(1)} %get-tuple-element.32, bf16[1,80,9,640]{3,1,0,2:T(8,128)(2,1)S(1)} %bitcast.38), kind=kLoop, calls=%fused_computation | loop fusion | flops 2764800 | bytes 5529600 | tf_op jit(solution)/shard_map/transpose | solution.py:548
  11.6 138.7 %shard_map.93 = (bf16[4,16,16,640]{3,2,1,0:T(8,128)(2,1)}, bf16[9,80,640]{2,1,0:T(8,128)(2,1)}, bf16[9,3,80,640]{3,2,1,0:T(8,128)(2,1)}, bf16[9,80,640]{2,1,0:T(8,128)(2,1)}) custom-call(f32[2]{0:T(128)} %add_convert_fusion.flags, bf16[4,16,16,640]{3,2,1,0:T(8,128)(2,1)} %bitcast.48, bf16[4,16,16,640]{3,2,1,0:T(8,128)(2,1)} %bitcast.49, ...), custom_call_target="tpu_custom_call" | custom-call | flops 22649241600 | bytes 16000000 | tf_op jit(solution)/shard_map/pallas_call | solution.py:555
  150.3 1.3 convert_bitcast_fusion.3
  151.7 0.7 copy.15
  152.4 1.4 reshape.113
  153.8 3.9 %convert_bitcast_fusion = (f32[80,9,640]{2,0,1:T(8,128)S(1)}, f32[80,9,640]{2,0,1:T(8,128)}, f32[80,9,640]{2,0,1:T(8,128)}) fusion(bf16[9,3,80,640]{3,2,1,0:T(8,128)(2,1)} %get-tuple-element.11), kind=kLoop, calls=%fused_computation.3 | loop fusion | flops 1382400 | bytes 8294400 | tf_op jit(solution)/shard_map/reshape | solution.py:599
  157.7 0.7 copy.16
  158.5 1.4 reshape.115
  159.9 2.2 %copy.14 = f32[80,9,640]{2,1,0:T(8,128)S(1)} copy(f32[80,9,640]{2,0,1:T(8,128)} %get-tuple-element.29) | data formatting | bytes 3686400 | tf_op jit(solution)/shard_map/reshape | solution.py:599
  162.1 1.4 reshape.111
  163.6 2.2 %copy.13 = f32[80,9,640]{2,1,0:T(8,128)S(1)} copy(f32[80,9,640]{2,0,1:T(8,128)} %get-tuple-element.30) | data formatting | bytes 3686400 | tf_op jit(solution)/shard_map/reshape | solution.py:599
  165.8 1.4 reshape.109
  167.2 0.0 copy-start.2
  167.2 6.5 %divide_subtract_fusion = (f32[1,80,5760]{2,1,0:T(8,128)}, f32[1,80,5760]{2,1,0:T(8,128)}, f32[1,80,5760]{2,1,0:T(8,128)}) fusion(f32[1,80,5760]{2,1,0:T(8,128)} %reshape.109, f32[1,80,5760]{2,1,0:T(8,128)} %param.8, pred[]{:T(512)S(6)} %and.4, f32[1,80,5760]{2,1,0:T(8,128)} %reshape.113, f32[1,80,5760]{2,1,0:T(8,128)} %reshape.111, f32[1,80,5760]{2,1,0:T(8,128)} %param.9, ...), kind=kLoop, calls=%fused_computation.7 | loop fusion | flops 6912000 | bytes 18432000 | tf_op jit(solution)/shard_map/sub | solution.py:87
  173.8 0.0 copy-done.2
  173.8 1.1 copy.25
  (1 shorter events, 0.0 us)
Async XLA Ops:
  6.0 2.1 %copy-start.1 = (f32[1,80,5760]{2,1,0:T(8,128)S(1)}, f32[1,80,5760]{2,1,0:T(8,128)}, u32[]{:S(2)}) copy-start(f32[1,80,5760]{2,1,0:T(8,128)} %param.9) | copy-start | bytes 5529604
  7.8 1.6 copy-start
  167.2 6.6 %copy-start.2 = (bf16[4,16,16,640]{3,2,1,0:T(8,128)(2,1)S(1)}, bf16[4,16,16,640]{3,2,1,0:T(8,128)(2,1)}, u32[]{:S(2)}) copy-start(bf16[4,16,16,640]{3,2,1,0:T(8,128)(2,1)} %get-tuple-element.10) | copy-start | bytes 3932164
where the time goes:
time: 175 us
  Pallas kernels  139 us (79%)
  other arithmetic  17.6 us (10%)
  local copies, waits for them, and re-layouts  15.7 us (9%)
  between operations  2.8 us (2%)
    pallas_call x1, Pallas kernels, local_block(): pl.pallas_call(block_kernel, out_shape=(jax.ShapeDtypeStruct(latents.shap...  139 us
    reshape x8, local copies, waits for them, and re-layouts, flat(): return taps.astype(jnp.float32).transpose(1, 0, 2).reshape(rows, 9 * width)  11.6 us
    sub x1, other arithmetic, adam_update(): weights_now - RATE * (first_new / first_fix) / (jnp.sqrt(second_new / sec...  6.55 us
    reshape x2, other arithmetic, flat(): return taps.astype(jnp.float32).transpose(1, 0, 2).reshape(rows, 9 * width)  5.25 us

commit v1 on v0

--- a/solution.py
+++ b/solution.py
@@ -163,14 +163,21 @@
 
 
 def block_kernel(
-    flags,
+    sources,
     latents,
+    weights,
+    cotangent_hbm,
+    first_hbm,
+    second_hbm,
+    latent_grad,
+    grad_out,
+    weights_out,
+    first_out,
+    second_out,
     cotangent,
-    state,
-    latent_grad,
+    first_moment,
+    second_moment,
     grad,
-    arrived,
-    moved,
     kall,
     near,
     act_t,
@@ -194,11 +201,12 @@
     rs_recv,
     z_send,
     z_recv,
+    load_sem,
 ):
     images, side = latents.shape[0], latents.shape[1]
     width = latents.shape[3]
     cells = side * side
-    rows = state.shape[2]
+    rows = weights.shape[0]
     scale = (9 * CH_IN) ** (-0.5)
     f32, bf16 = jnp.float32, jnp.bfloat16
     k = lax.axis_index("member")
@@ -208,8 +216,27 @@
     xp = me + 2 - 4 * x
     yp = me + 4 - 8 * y
     diag = xp + 4 - 8 * y
-    named = flags[0]
-    from_below = flags[1]
+    loads = [
+        pltpu.make_async_copy(src, dst, load_sem.at[at])
+        for at, (src, dst) in enumerate(
+            (
+                (first_hbm, first_moment),
+                (second_hbm, second_moment),
+                (cotangent_hbm, cotangent),
+            )
+        )
+    ]
+    for load in loads:
+        load.start()
+    named = jnp.float32(0.0)
+    from_below = jnp.float32(0.0)
+    taking = jnp.float32(0.0)
+    for member in range(4):
+        source = sources[member]
+        takes = jnp.where(source != member, 1.0, 0.0)
+        named += takes * jnp.where(source == k, 1.0, 0.0)
+        from_below += takes * jnp.where(source < member, 1.0, 0.0)
+        taking += takes * jnp.where(k == member, 1.0, 0.0)
 
     def remote(src, dst, send, recv, member, index):
         return pltpu.make_async_remote_copy(
@@ -270,22 +297,30 @@
             part = block(t, (xp + over, yp + over, diag + over)[kind - 5])
         return remote(part, part, ag_send.at[t, kind], ag_recv.at[t, kind], k, sib)
 
+    state = (weights, first_moment, second_moment)
+
+    def columns(t):
+        return pl.ds(pl.multiple_of(t * width, 128), width)
+
     def state_step(tick, lane, rank, here, target):
-        j = tick // 2 - 2 * rank
-
-        @pl.when((tick % 2 == 0) & (j >= 0) & (j < 9) & (rank < 3))
+        j = jnp.where(rank == 0, tick, tick // 2 - 2 * rank)
+        even = (tick % 2 == 0) | (rank == 0)
+
+        @pl.when(even & (j >= 0) & (j < 9) & (rank < 3))
         def _():
             @pl.when(rank == 0)
             def _():
-                here[j] = state[j]
+                for at in range(3):
+                    here[j, at] = state[at][:, columns(j)].astype(bf16)
 
             @pl.when(rank > 0)
             def _():
                 remote(
                     here.at[j], here.at[j], z_send.at[lane, j], z_recv.at[lane, j], target, me
                 ).wait_recv()
-                mine, came = state[j].astype(f32), here[j].astype(f32)
-                here[j] = (mine * named + came * (1.0 - named)).astype(bf16)
+                for at in range(3):
+                    mine, came = state[at][:, columns(j)], here[j, at].astype(f32)
+                    here[j, at] = (mine * named + came * (1.0 - named)).astype(bf16)
 
             remote(
                 here.at[j], here.at[j], z_send.at[lane, j], z_recv.at[lane, j], target, me
@@ -320,7 +355,7 @@
             grad_step(tick, 3, 3 - k, down_grad, jnp.maximum(k - 1, 0))
 
     def cast_tap(t, carry):
-        kall[t, me] = state[t, 0]
+        kall[t, me] = weights[:, columns(t)].astype(bf16)
         return carry
 
     lax.fori_loop(0, 9, cast_tap, 0)
@@ -352,10 +387,12 @@
             near[at, b, i + 1] = moved_values.astype(bf16)
         return carry
 
-    lax.fori_loop(0, images * side, activate, 0)
-    for b in range(images):
+    def turn(b):
         flat = near[1, b, 1 : side + 1].reshape(cells, width)
-        act_t[:, b * cells : (b + 1) * cells] = jnp.transpose(flat)
+        act_t[b] = jnp.transpose(flat)
+
+    for load in loads:
+        load.wait()
 
     def forward(i, carry):
         @pl.when(i < 9)
@@ -379,6 +416,16 @@
             gather_wait(i - 1, 4)
             gather(i - 1, 7).start()
 
+        half_rows = images * side // 2
+
+        @pl.when(i < 2)
+        def _():
+            lax.fori_loop(i * half_rows, (i + 1) * half_rows, activate, 0)
+
+        @pl.when((i >= 2) & (i < 2 + images))
+        def _():
+            turn(i - 2)
+
         @pl.when(i >= 2)
         def _():
             t = i - 2
@@ -386,13 +433,16 @@
                 gather_wait(t, kind)
             weight = kall[t].reshape(8 * rows, width)
 
-            def one(b, carry):
-                window = near[t % 3, b, pl.ds(t // 3, side)].reshape(cells, width)
-                product = jnp.dot(window, weight, preferred_element_type=f32)
-                total[b] = jnp.where(t == 0, 0.0, total[b]) + product
-                return carry
-
-            lax.fori_loop(0, images, one, 0)
+            window = near[t % 3, :, pl.ds(t // 3, side)].reshape(images * cells, width)
+            product = jnp.dot(window, weight, preferred_element_type=f32)
+
+            @pl.when(t == 0)
+            def _():
+                total[...] = product
+
+            @pl.when(t > 0)
+            def _():
+                total[...] += product
 
         return carry
 
@@ -400,16 +450,13 @@
 
     def slope_rows(n, carry):
         b, i = n // side, n % side
-        hidden = scale * total[b, pl.ds(pl.multiple_of(i * side, side), side)]
+        hidden = scale * total[pl.ds(pl.multiple_of(n * side, side), side)]
         value = cotangent[b, i].astype(f32) * silu_slope(hidden)
         for at, moved_values in enumerate(shifted(value)):
             near[at, b, i + 1] = moved_values.astype(bf16)
         return carry
 
-    lax.fori_loop(0, images * side, slope_rows, 0)
-
-    def window_of(t, b):
-        return near[2 - t % 3, b, pl.ds(2 - t // 3, side)].reshape(cells, width)
+    lax.fori_loop(0, images * side, slope_rows, 0, unroll=4)
 
     def scatter(t, kind):
         if kind == 0:
@@ -462,57 +509,84 @@
         member_steps(t + 9, True)
         window = near[2 - t % 3, :, pl.ds(2 - t // 3, side)].reshape(images * cells, width)
 
-        def one(yy, carry):
-            lhs = act_t[pl.ds(pl.multiple_of(yy * 4 * rows, 64), 4 * rows)]
-            product = scale * jnp.dot(lhs, window, preferred_element_type=f32)
-            partial[t, yy] = product.astype(bf16).reshape(2, 2, rows, width)
-            return carry
-
-        lax.fori_loop(0, 2, one, 0)
+        lhs = jnp.concatenate([act_t[b] for b in range(images)], axis=1)
+        product = scale * jnp.dot(lhs, window, preferred_element_type=f32)
+        partial[t] = product.astype(bf16).reshape(2, 2, 2, rows, width)
         scatter(t, 0).start()
         return carry
 
     lax.fori_loop(0, 9, kernel_grad, 0)
 
-    def back(t, carry):
-        scatter_steps(t + 9)
-        member_steps(t + 18, True)
-        weight = kall[t].reshape(8 * rows, width)
-
-        def one(b, carry):
+    def back(r, carry):
+        def tick(col):
+            scatter_steps(3 * r + col + 9)
+            member_steps(3 * r + col + 18, True)
+
+        weight = jnp.concatenate(
+            [kall[3 * r + col].reshape(8 * rows, width) for col in range(3)], axis=1
+        )
+        pair = images // 2
+        for part in range(2):
+            windows = jnp.concatenate(
+                [
+                    near[2 - col, part * pair : (part + 1) * pair, pl.ds(2 - r, side)].reshape(
+                        pair * cells, width
+                    )
+                    for col in range(3)
+                ],
+                axis=1,
+            )
             product = lax.dot_general(
-                window_of(t, b), weight, (((1,), (1,)), ((), ())), preferred_element_type=f32
+                windows, weight, (((1,), (1,)), ((), ())), preferred_element_type=f32
             )
-            total[b] = jnp.where(t == 0, 0.0, total[b]) + product
-            return carry
-
-        lax.fori_loop(0, images, one, 0)
-        return carry
-
-    lax.fori_loop(0, 9, back, 0)
+            here = pl.ds(part * pair * cells, pair * cells)
+
+            @pl.when(r == 0)
+            def _():
+                total[here] = product
+
+            @pl.when(r > 0)
+            def _():
+                total[here] += product
+
+            tick(part)
+        tick(2)
+        return carry
+
+    lax.fori_loop(0, 3, back, 0)
 
     def finish(n, carry):
         b, i = n // side, n % side
-        value = scale * total[b, pl.ds(pl.multiple_of(i * side, side), side)]
+        value = scale * total[pl.ds(pl.multiple_of(n * side, side), side)]
         value = value * silu_slope(latents[b, i].astype(f32))
         latent_grad[b, i] = value.astype(bf16)
         return carry
 
-    lax.fori_loop(0, images * side, finish, 0)
-
-    def pick(dst, below, above, j):
+    lax.fori_loop(0, images * side, finish, 0, unroll=4)
+
+    def mix(lower, upper, share):
+        return (lower.astype(f32) * share + upper.astype(f32) * (1.0 - share)).astype(bf16)
+
+    def pick(j):
+        def store(below, above, share):
+            for at, out in enumerate((weights_out, first_out, second_out)):
+                out[:, columns(j)] = mix(below[0][j, at], above[0][j, at], share)
+            came = mix(below[1][j], above[1][j], share)
+            grad_out[:, columns(j)] = mix(came, grad[j], taking)
+
+        low, high = (up_in, up_grad), (down_in, down_grad)
+
         @pl.when(k == 0)
         def _():
-            dst[j] = above[j]
+            store(high, high, 1.0)
 
         @pl.when(k == 3)
         def _():
-            dst[j] = below[j]
+            store(low, low, 1.0)
 
         @pl.when((k > 0) & (k < 3))
         def _():
-            lower, upper = below[j].astype(f32), above[j].astype(f32)
-            dst[j] = (lower * from_below + upper * (1.0 - from_below)).astype(bf16)
+            store(low, high, from_below)
 
     def drain(j, carry):
         for lane, here in enumerate((up_in, down_in, up_grad, down_grad)):
@@ -527,8 +601,7 @@
             def _():
                 copy.wait_send()
 
-        pick(arrived, up_in, down_in, j)
-        pick(moved, up_grad, down_grad, j)
+        pick(j)
         for kind in range(8):
             gather(j, kind).wait_send()
         for kind in range(5):
@@ -540,33 +613,34 @@
 
 def local_block(latents, cotangent, weights, first_moment, second_moment, sources):
     me = lax.axis_index("member")
-    takers, named = takers_and_named(sources)
-    taker, source = takers[0], named[0]
+    members = jnp.arange(4, dtype=jnp.int32)
+    taking = jnp.any((sources != members) & (members == me))
     rows, width = weights.shape[1], latents.shape[4]
     bf16 = jnp.bfloat16
-    state = jnp.stack([weights[0], first_moment[0], second_moment[0]]).astype(bf16)
-    state = state.reshape(3, rows, 9, width).transpose(2, 0, 1, 3)
-    flags = jnp.stack([source == me, source < taker]).astype(jnp.float32)
+    flat = (rows, 9 * width)
     images, side = latents.shape[1], latents.shape[2]
     cells = side * side
     vmem = pl.BlockSpec(memory_space=pltpu.VMEM)
     tap = (9, rows, width)
     half, rest = HALF, rows - HALF
-    latent_grad, grad, arrived, moved = pl.pallas_call(
+    latent_grad, grad, weights_in, first_in, second_in = pl.pallas_call(
         block_kernel,
         out_shape=(
             jax.ShapeDtypeStruct(latents.shape[1:], bf16),
-            jax.ShapeDtypeStruct(tap, bf16),
-            jax.ShapeDtypeStruct((9, 3, rows, width), bf16),
-            jax.ShapeDtypeStruct(tap, bf16),
-        ),
-        in_specs=[pl.BlockSpec(memory_space=pltpu.SMEM), vmem, vmem, vmem],
-        out_specs=(vmem,) * 4,
+        )
+        + (jax.ShapeDtypeStruct(flat, bf16),) * 4,
+        in_specs=[pl.BlockSpec(memory_space=pltpu.SMEM), vmem, vmem]
+        + [pl.BlockSpec(memory_space=pl.ANY)] * 3,
+        out_specs=(vmem,) * 5,
         scratch_shapes=[
+            pltpu.VMEM(latents.shape[1:], bf16),
+            pltpu.VMEM(flat, jnp.float32),
+            pltpu.VMEM(flat, jnp.float32),
+            pltpu.VMEM(tap, bf16),
             pltpu.VMEM((9, 8, rows, width), bf16),
             pltpu.VMEM((3, images, side + 2, side, width), bf16),
-            pltpu.VMEM((width, images * cells), bf16),
-            pltpu.VMEM((images, cells, width), jnp.float32),
+            pltpu.VMEM((images, width, cells), bf16),
+            pltpu.VMEM((images * cells, width), jnp.float32),
             pltpu.VMEM((9, 2, 2, 2, rows, width), bf16),
             pltpu.VMEM((9, 2, 2, rows, width), bf16),
             pltpu.VMEM((9, 2, 2, rows, width), bf16),
@@ -586,6 +660,7 @@
             pltpu.SemaphoreType.DMA((9, 5)),
             pltpu.SemaphoreType.DMA((4, 9)),
             pltpu.SemaphoreType.DMA((4, 9)),
+            pltpu.SemaphoreType.DMA((3,)),
         ],
         compiler_params=pltpu.CompilerParams(
             collective_id=0, has_side_effects=True, vmem_limit_bytes=60 * 1024 * 1024
@@ -593,16 +668,13 @@
         cost_estimate=pl.CostEstimate(
             flops=6 * images * cells * 9 * width * width, bytes_accessed=16000000, transcendentals=0
         ),
-    )(flags, latents[0], cotangent[0], state)
-
-    def flat(taps):
-        return taps.astype(jnp.float32).transpose(1, 0, 2).reshape(rows, 9 * width)
-
-    taking = (taker == me) & (source != me)
-    weights_now = jnp.where(taking, flat(arrived[:, 0]), weights[0])
-    first_now = jnp.where(taking, flat(arrived[:, 1]), first_moment[0])
-    second_now = jnp.where(taking, flat(arrived[:, 2]), second_moment[0])
-    gradient = flat(jnp.where(taking, moved, grad))
+    )(sources, latents[0], weights[0], cotangent[0], first_moment[0], second_moment[0])
+
+    f32 = jnp.float32
+    weights_now = jnp.where(taking, weights_in.astype(f32), weights[0])
+    first_now = jnp.where(taking, first_in.astype(f32), first_moment[0])
+    second_now = jnp.where(taking, second_in.astype(f32), second_moment[0])
+    gradient = grad.astype(f32)
     updated, first_new, second_new = adam_update(weights_now, first_now, second_now, gradient)
     return (latent_grad[None], updated[None], first_new[None], second_new[None])
 

time: 175 us -> 144 us (0.82)
  local copies, waits for them, and re-layouts: 15.7 us -> 1.07 us
  other arithmetic: 17.6 us -> 8.67 us
  Pallas kernels: 139 us -> 133 us
  between operations: 2.8 us -> 0.67 us
    reshape x8 -> x0, local copies, waits for them, and re-layouts: 11.6 us -> none  [flat(): return taps.astype(jnp.float32).transpose(1, 0, 2).reshape(rows, 9 * width)]
    broadcast_in_dim x0 -> x1, other arithmetic: none -> 7.37 us  [local_block(): return (latent_grad[None], updated[None], first_new[None], second_new[None])]
    sub x1 -> x0, other arithmetic: 6.55 us -> none  [adam_update(): weights_now - RATE * (first_new / first_fix) / (jnp.sqrt(second_new / sec...]
    pallas_call x1, Pallas kernels: 139 us -> 133 us  [local_block(): pl.pallas_call(block_kernel, out_shape=(jax.ShapeDtypeStruct(latents.shap...]
    reshape x2 -> x0, other arithmetic: 5.25 us -> none  [flat(): return taps.astype(jnp.float32).transpose(1, 0, 2).reshape(rows, 9 * width)]
    another operation x3 -> x0, other arithmetic: 1.93 us -> none
    transpose x1 -> x0, other arithmetic: 1.9 us -> none  [local_block(): state = state.reshape(3, rows, 9, width).transpose(2, 0, 1, 3)]
where the time goes in v1:
time: 144 us
  Pallas kernels  133 us (92%)
  other arithmetic  8.67 us (6%)
    pallas_call x1, Pallas kernels, local_block(): pl.pallas_call(block_kernel, out_shape=(jax.ShapeDtypeStruct(latents.shap...  133 us
    broadcast_in_dim x1, other arithmetic, local_block(): return (latent_grad[None], updated[None], first_new[None], second_new[None])  7.37 us

profile of v1, /device:TPU:0, one launch (start us, length us, event | category | flops | bytes accessed | tf_op | source)
XLA Modules:
  0.0 143.7 jit_solution(923025004588859974)
XLA Ops:
  0.6 1.3 and_reduce_fusion
  1.9 0.0 copy-start
  1.9 0.0 copy-start.1
  1.9 133.3 %shard_map.93 = (bf16[4,16,16,640]{3,2,1,0:T(8,128)(2,1)}, bf16[80,5760]{1,0:T(8,128)(2,1)}, bf16[80,5760]{1,0:T(8,128)(2,1)}, bf16[80,5760]{1,0:T(8,128)(2,1)}, bf16[80,5760]{1,0:T(8,128)(2,1)}) custom-call(s32[4]{0:T(128)} %sources.1, bf16[4,16,16,640]{3,2,1,0:T(8,128)(2,1)} %bitcast.21, f32[80,5760]{1,0:T(8,128)} %bitcast.17, ...), custom_call_target="tpu_custom_call" | custom-call | flops 22649241600 | bytes 16000000 | tf_op jit(solution)/shard_map/pallas_call | solution.py:626
  135.3 0.0 copy-done
  135.3 0.0 copy-done.1
  135.3 0.0 copy-start.2
  135.3 7.4 %fusion.3 = (f32[1,80,5760]{2,1,0:T(8,128)}, f32[1,80,5760]{2,1,0:T(8,128)}, f32[1,80,5760]{2,1,0:T(8,128)}) fusion(bf16[80,5760]{1,0:T(8,128)(2,1)} %get-tuple-element.12, bf16[80,5760]{1,0:T(8,128)(2,1)} %get-tuple-element.13, pred[]{:T(512)} %and_reduce_fusion, f32[1,80,5760]{2,1,0:T(8,128)} %param.10, f32[1,80,5760]{2,1,0:T(8,128)S(1)} %copy-done.1, ...), kind=kLoop, calls=%fused_computation.6 | loop fusion | flops 8755200 | bytes 14745601 | tf_op jit(solution)/shard_map/broadcast_in_dim | solution.py:679
  142.7 0.0 copy-done.2
  142.7 1.1 copy.11
Async XLA Ops:
  1.9 133.3 %copy-start = (f32[1,80,5760]{2,1,0:T(8,128)S(1)}, f32[1,80,5760]{2,1,0:T(8,128)}, u32[]{:S(2)}) copy-start(f32[1,80,5760]{2,1,0:T(8,128)} %param.8) | copy-start | bytes 5529604
  1.9 133.4 %copy-start.1 = (f32[1,80,5760]{2,1,0:T(8,128)S(1)}, f32[1,80,5760]{2,1,0:T(8,128)}, u32[]{:S(2)}) copy-start(f32[1,80,5760]{2,1,0:T(8,128)} %param.9) | copy-start | bytes 5529604
  135.3 7.4 %copy-start.2 = (bf16[4,16,16,640]{3,2,1,0:T(8,128)(2,1)S(1)}, bf16[4,16,16,640]{3,2,1,0:T(8,128)(2,1)}, u32[]{:S(2)}) copy-start(bf16[4,16,16,640]{3,2,1,0:T(8,128)(2,1)} %get-tuple-element.9) | copy-start | bytes 3932164

commit v2 on v1

--- a/solution.py
+++ b/solution.py
@@ -303,10 +303,10 @@
         return pl.ds(pl.multiple_of(t * width, 128), width)
 
     def state_step(tick, lane, rank, here, target):
-        j = jnp.where(rank == 0, tick, tick // 2 - 2 * rank)
-        even = (tick % 2 == 0) | (rank == 0)
-
-        @pl.when(even & (j >= 0) & (j < 9) & (rank < 3))
+        j = jnp.where(rank == 0, tick, (tick - 1) // 2 - rank)
+        due = (tick % 2 == 1) | (rank == 0)
+
+        @pl.when(due & (j >= 0) & (j < 9) & (rank < 3))
         def _():
             @pl.when(rank == 0)
             def _():
@@ -327,7 +327,7 @@
             ).start()
 
     def grad_step(tick, lane, rank, here, target):
-        t = tick - 14 - 2 * rank
+        t = tick - 16 - 2 * rank
 
         @pl.when((t >= 0) & (t < 9) & (rank < 3))
         def _():
@@ -395,9 +395,7 @@
         load.wait()
 
     def forward(i, carry):
-        @pl.when(i < 9)
-        def _():
-            member_steps(i, False)
+        member_steps(i, False)
 
         @pl.when(i + 4 < 9)
         def _():
@@ -420,7 +418,7 @@
 
         @pl.when(i < 2)
         def _():
-            lax.fori_loop(i * half_rows, (i + 1) * half_rows, activate, 0)
+            lax.fori_loop(0, half_rows, lambda n, carry: activate(n + i * half_rows, carry), 0, unroll=4)
 
         @pl.when((i >= 2) & (i < 2 + images))
         def _():
@@ -506,7 +504,7 @@
 
     def kernel_grad(t, carry):
         scatter_steps(t)
-        member_steps(t + 9, True)
+        member_steps(t + 11, True)
         window = near[2 - t % 3, :, pl.ds(2 - t // 3, side)].reshape(images * cells, width)
 
         lhs = jnp.concatenate([act_t[b] for b in range(images)], axis=1)
@@ -520,7 +518,7 @@
     def back(r, carry):
         def tick(col):
             scatter_steps(3 * r + col + 9)
-            member_steps(3 * r + col + 18, True)
+            member_steps(3 * r + col + 20, True)
 
         weight = jnp.concatenate(
             [kall[3 * r + col].reshape(8 * rows, width) for col in range(3)], axis=1
@@ -562,53 +560,64 @@
         latent_grad[b, i] = value.astype(bf16)
         return carry
 
-    lax.fori_loop(0, images * side, finish, 0, unroll=4)
-
     def mix(lower, upper, share):
         return (lower.astype(f32) * share + upper.astype(f32) * (1.0 - share)).astype(bf16)
 
-    def pick(j):
+    low, high = (up_in, up_grad), (down_in, down_grad)
+
+    def by_place(store):
+        @pl.when(k == 0)
+        def _():
+            store(high, high, 1.0)
+
+        @pl.when(k == 3)
+        def _():
+            store(low, low, 1.0)
+
+        @pl.when((k > 0) & (k < 3))
+        def _():
+            store(low, high, from_below)
+
+    def settle(lanes, j):
+        for lane, here in lanes:
+            copy = remote(here.at[j], here.at[j], z_send.at[lane, j], z_recv.at[lane, j], k, sib)
+            last = k == 3 if lane % 2 == 0 else k == 0
+
+            @pl.when(last)
+            def _():
+                copy.wait_recv()
+
+            @pl.when(jnp.logical_not(last))
+            def _():
+                copy.wait_send()
+
+    def drain_state(j, carry):
+        settle(((0, up_in), (1, down_in)), j)
+
         def store(below, above, share):
             for at, out in enumerate((weights_out, first_out, second_out)):
                 out[:, columns(j)] = mix(below[0][j, at], above[0][j, at], share)
-            came = mix(below[1][j], above[1][j], share)
-            grad_out[:, columns(j)] = mix(came, grad[j], taking)
-
-        low, high = (up_in, up_grad), (down_in, down_grad)
-
-        @pl.when(k == 0)
-        def _():
-            store(high, high, 1.0)
-
-        @pl.when(k == 3)
-        def _():
-            store(low, low, 1.0)
-
-        @pl.when((k > 0) & (k < 3))
-        def _():
-            store(low, high, from_below)
-
-    def drain(j, carry):
-        for lane, here in enumerate((up_in, down_in, up_grad, down_grad)):
-            copy = remote(here.at[j], here.at[j], z_send.at[lane, j], z_recv.at[lane, j], k, sib)
-            last = k == 3 if lane % 2 == 0 else k == 0
-
-            @pl.when(last)
-            def _():
-                copy.wait_recv()
-
-            @pl.when(jnp.logical_not(last))
-            def _():
-                copy.wait_send()
-
-        pick(j)
+
+        by_place(store)
         for kind in range(8):
             gather(j, kind).wait_send()
         for kind in range(5):
             scatter(j, kind).wait_send()
         return carry
 
-    lax.fori_loop(0, 9, drain, 0)
+    def drain_grad(j, carry):
+        settle(((2, up_grad), (3, down_grad)), j)
+
+        def store(below, above, share):
+            came = mix(below[1][j], above[1][j], share)
+            grad_out[:, columns(j)] = mix(came, grad[j], taking)
+
+        by_place(store)
+        return carry
+
+    lax.fori_loop(0, 9, drain_state, 0)
+    lax.fori_loop(0, images * side, finish, 0, unroll=4)
+    lax.fori_loop(0, 9, drain_grad, 0)
 
 
 def local_block(latents, cotangent, weights, first_moment, second_moment, sources):

time: 144 us -> 132 us (0.917)
  Pallas kernels: 133 us -> 121 us
    pallas_call x1, Pallas kernels: 133 us -> 121 us  [local_block(): pl.pallas_call(block_kernel, out_shape=(jax.ShapeDtypeStruct(latents.shap...]
where the time goes in v2:
time: 132 us; the launch traced here: 131 us
  Pallas kernels  121 us (92%)
  other arithmetic  8.67 us (7%)
    pallas_call x1, Pallas kernels, local_block(): pl.pallas_call(block_kernel, out_shape=(jax.ShapeDtypeStruct(latents.shap...  121 us
    broadcast_in_dim x1, other arithmetic, local_block(): return (latent_grad[None], updated[None], first_new[None], second_new[None])  7.37 us

profile of v2, /device:TPU:0, one launch (start us, length us, event | category | flops | bytes accessed | tf_op | source)
XLA Modules:
  0.0 131.3 jit_solution(8065701741329372542)
XLA Ops:
  0.6 1.3 and_reduce_fusion
  1.9 0.0 copy-start
  1.9 0.0 copy-start.1
  1.9 120.9 %shard_map.93 = (bf16[4,16,16,640]{3,2,1,0:T(8,128)(2,1)}, bf16[80,5760]{1,0:T(8,128)(2,1)}, bf16[80,5760]{1,0:T(8,128)(2,1)}, bf16[80,5760]{1,0:T(8,128)(2,1)}, bf16[80,5760]{1,0:T(8,128)(2,1)}) custom-call(s32[4]{0:T(128)} %sources.1, bf16[4,16,16,640]{3,2,1,0:T(8,128)(2,1)} %bitcast.21, f32[80,5760]{1,0:T(8,128)} %bitcast.17, ...), custom_call_target="tpu_custom_call" | custom-call | flops 22649241600 | bytes 16000000 | tf_op jit(solution)/shard_map/pallas_call | solution.py:635
  122.9 0.0 copy-done
  122.9 0.0 copy-done.1
  122.9 0.0 copy-start.2
  122.9 7.4 %fusion.3 = (f32[1,80,5760]{2,1,0:T(8,128)}, f32[1,80,5760]{2,1,0:T(8,128)}, f32[1,80,5760]{2,1,0:T(8,128)}) fusion(bf16[80,5760]{1,0:T(8,128)(2,1)} %get-tuple-element.12, bf16[80,5760]{1,0:T(8,128)(2,1)} %get-tuple-element.13, pred[]{:T(512)} %and_reduce_fusion, f32[1,80,5760]{2,1,0:T(8,128)} %param.10, f32[1,80,5760]{2,1,0:T(8,128)S(1)} %copy-done.1, ...), kind=kLoop, calls=%fused_computation.6 | loop fusion | flops 8755200 | bytes 14745601 | tf_op jit(solution)/shard_map/broadcast_in_dim | solution.py:688
  130.3 0.0 copy-done.2
  130.3 1.1 copy.11
Async XLA Ops:
  1.9 121.0 %copy-start = (f32[1,80,5760]{2,1,0:T(8,128)S(1)}, f32[1,80,5760]{2,1,0:T(8,128)}, u32[]{:S(2)}) copy-start(f32[1,80,5760]{2,1,0:T(8,128)} %param.8) | copy-start | bytes 5529604
  1.9 121.0 %copy-start.1 = (f32[1,80,5760]{2,1,0:T(8,128)S(1)}, f32[1,80,5760]{2,1,0:T(8,128)}, u32[]{:S(2)}) copy-start(f32[1,80,5760]{2,1,0:T(8,128)} %param.9) | copy-start | bytes 5529604
  122.9 7.4 %copy-start.2 = (bf16[4,16,16,640]{3,2,1,0:T(8,128)(2,1)S(1)}, bf16[4,16,16,640]{3,2,1,0:T(8,128)(2,1)}, u32[]{:S(2)}) copy-start(bf16[4,16,16,640]{3,2,1,0:T(8,128)(2,1)} %get-tuple-element.9) | copy-start | bytes 3932164

commit v3 on v2

--- a/solution.py
+++ b/solution.py
@@ -302,29 +302,29 @@
     def columns(t):
         return pl.ds(pl.multiple_of(t * width, 128), width)
 
+    def state_copy(lane, here, j, at, target):
+        part = here.at[j, at]
+        n = 3 * j + at
+        return remote(part, part, z_send.at[lane, n], z_recv.at[lane, n], target, me)
+
     def state_step(tick, lane, rank, here, target):
-        j = jnp.where(rank == 0, tick, (tick - 1) // 2 - rank)
-        due = (tick % 2 == 1) | (rank == 0)
-
-        @pl.when(due & (j >= 0) & (j < 9) & (rank < 3))
-        def _():
-            @pl.when(rank == 0)
+        @pl.when((rank == 0) & (tick < 9))
+        def _():
+            for at in range(3):
+                here[tick, at] = state[at][:, columns(tick)].astype(bf16)
+                state_copy(lane, here, tick, at, target).start()
+
+        for at in range(3):
+            since = tick - at - rank
+
+            @pl.when((since >= 0) & (since % 2 == 0) & (since < 18) & (rank > 0) & (rank < 3))
             def _():
-                for at in range(3):
-                    here[j, at] = state[at][:, columns(j)].astype(bf16)
-
-            @pl.when(rank > 0)
-            def _():
-                remote(
-                    here.at[j], here.at[j], z_send.at[lane, j], z_recv.at[lane, j], target, me
-                ).wait_recv()
-                for at in range(3):
-                    mine, came = state[at][:, columns(j)], here[j, at].astype(f32)
-                    here[j, at] = (mine * named + came * (1.0 - named)).astype(bf16)
-
-            remote(
-                here.at[j], here.at[j], z_send.at[lane, j], z_recv.at[lane, j], target, me
-            ).start()
+                j = since // 2
+                copy = state_copy(lane, here, j, at, target)
+                copy.wait_recv()
+                mine, came = state[at][:, columns(j)], here[j, at].astype(f32)
+                here[j, at] = (mine * named + came * (1.0 - named)).astype(bf16)
+                copy.start()
 
     def grad_step(tick, lane, rank, here, target):
         t = tick - 16 - 2 * rank
@@ -578,21 +578,21 @@
         def _():
             store(low, high, from_below)
 
-    def settle(lanes, j):
-        for lane, here in lanes:
-            copy = remote(here.at[j], here.at[j], z_send.at[lane, j], z_recv.at[lane, j], k, sib)
-            last = k == 3 if lane % 2 == 0 else k == 0
-
-            @pl.when(last)
-            def _():
-                copy.wait_recv()
-
-            @pl.when(jnp.logical_not(last))
-            def _():
-                copy.wait_send()
+    def settle(lane, copy):
+        last = k == 3 if lane % 2 == 0 else k == 0
+
+        @pl.when(last)
+        def _():
+            copy.wait_recv()
+
+        @pl.when(jnp.logical_not(last))
+        def _():
+            copy.wait_send()
 
     def drain_state(j, carry):
-        settle(((0, up_in), (1, down_in)), j)
+        for lane, here in ((0, up_in), (1, down_in)):
+            for at in range(3):
+                settle(lane, state_copy(lane, here, j, at, k))
 
         def store(below, above, share):
             for at, out in enumerate((weights_out, first_out, second_out)):
@@ -606,7 +606,9 @@
         return carry
 
     def drain_grad(j, carry):
-        settle(((2, up_grad), (3, down_grad)), j)
+        for lane, here in ((2, up_grad), (3, down_grad)):
+            part = here.at[j]
+            settle(lane, remote(part, part, z_send.at[lane, j], z_recv.at[lane, j], k, sib))
 
         def store(below, above, share):
             came = mix(below[1][j], above[1][j], share)
@@ -667,8 +669,8 @@
             pltpu.SemaphoreType.DMA((9, 8)),
             pltpu.SemaphoreType.DMA((9, 5)),
             pltpu.SemaphoreType.DMA((9, 5)),
-            pltpu.SemaphoreType.DMA((4, 9)),
-            pltpu.SemaphoreType.DMA((4, 9)),
+            pltpu.SemaphoreType.DMA((4, 27)),
+            pltpu.SemaphoreType.DMA((4, 27)),
             pltpu.SemaphoreType.DMA((3,)),
         ],
         compiler_params=pltpu.CompilerParams(

time: 132 us -> 143 us (1.083)
  Pallas kernels: 121 us -> 133 us
    pallas_call x1, Pallas kernels: 121 us -> 133 us  [local_block(): pl.pallas_call(block_kernel, out_shape=(jax.ShapeDtypeStruct(latents.shap...]
where the time goes in v3:
time: 143 us
  Pallas kernels  133 us (93%)
  other arithmetic  8.67 us (6%)
    pallas_call x1, Pallas kernels, local_block(): pl.pallas_call(block_kernel, out_shape=(jax.ShapeDtypeStruct(latents.shap...  133 us
    broadcast_in_dim x1, other arithmetic, local_block(): return (latent_grad[None], updated[None], first_new[None], second_new[None])  7.37 us

profile of v3, /device:TPU:0, one launch (start us, length us, event | category | flops | bytes accessed | tf_op | source)
XLA Modules:
  0.0 143.2 jit_solution(12453428751226451645)
XLA Ops:
  0.6 1.3 and_reduce_fusion
  1.9 0.0 copy-start
  1.9 0.0 copy-start.1
  1.9 132.8 %shard_map.93 = (bf16[4,16,16,640]{3,2,1,0:T(8,128)(2,1)}, bf16[80,5760]{1,0:T(8,128)(2,1)}, bf16[80,5760]{1,0:T(8,128)(2,1)}, bf16[80,5760]{1,0:T(8,128)(2,1)}, bf16[80,5760]{1,0:T(8,128)(2,1)}) custom-call(s32[4]{0:T(128)} %sources.1, bf16[4,16,16,640]{3,2,1,0:T(8,128)(2,1)} %bitcast.21, f32[80,5760]{1,0:T(8,128)} %bitcast.17, ...), custom_call_target="tpu_custom_call" | custom-call | flops 22649241600 | bytes 16000000 | tf_op jit(solution)/shard_map/pallas_call | solution.py:637
  134.7 0.0 copy-done
  134.7 0.0 copy-done.1
  134.8 0.0 copy-start.2
  134.8 7.4 %fusion.3 = (f32[1,80,5760]{2,1,0:T(8,128)}, f32[1,80,5760]{2,1,0:T(8,128)}, f32[1,80,5760]{2,1,0:T(8,128)}) fusion(bf16[80,5760]{1,0:T(8,128)(2,1)} %get-tuple-element.12, bf16[80,5760]{1,0:T(8,128)(2,1)} %get-tuple-element.13, pred[]{:T(512)} %and_reduce_fusion, f32[1,80,5760]{2,1,0:T(8,128)} %param.10, f32[1,80,5760]{2,1,0:T(8,128)S(1)} %copy-done.1, ...), kind=kLoop, calls=%fused_computation.6 | loop fusion | flops 8755200 | bytes 14745601 | tf_op jit(solution)/shard_map/broadcast_in_dim | solution.py:690
  142.1 0.0 copy-done.2
  142.1 1.1 copy.11
Async XLA Ops:
  1.9 132.8 %copy-start = (f32[1,80,5760]{2,1,0:T(8,128)S(1)}, f32[1,80,5760]{2,1,0:T(8,128)}, u32[]{:S(2)}) copy-start(f32[1,80,5760]{2,1,0:T(8,128)} %param.8) | copy-start | bytes 5529604
  1.9 132.8 %copy-start.1 = (f32[1,80,5760]{2,1,0:T(8,128)S(1)}, f32[1,80,5760]{2,1,0:T(8,128)}, u32[]{:S(2)}) copy-start(f32[1,80,5760]{2,1,0:T(8,128)} %param.9) | copy-start | bytes 5529604
  134.8 7.4 %copy-start.2 = (bf16[4,16,16,640]{3,2,1,0:T(8,128)(2,1)S(1)}, bf16[4,16,16,640]{3,2,1,0:T(8,128)(2,1)}, u32[]{:S(2)}) copy-start(bf16[4,16,16,640]{3,2,1,0:T(8,128)(2,1)} %get-tuple-element.9) | copy-start | bytes 3932164

commit v4 on v2

--- a/solution.py
+++ b/solution.py
@@ -303,8 +303,8 @@
         return pl.ds(pl.multiple_of(t * width, 128), width)
 
     def state_step(tick, lane, rank, here, target):
-        j = jnp.where(rank == 0, tick, (tick - 1) // 2 - rank)
-        due = (tick % 2 == 1) | (rank == 0)
+        j = jnp.where(rank == 0, tick // 2, (tick - 1) // 2 - rank)
+        due = tick % 2 == jnp.where(rank == 0, 0, 1)
 
         @pl.when(due & (j >= 0) & (j < 9) & (rank < 3))
         def _():

time: 132 us -> 135 us (1.023)
  Pallas kernels: 121 us -> 124 us
    pallas_call x1, Pallas kernels: 121 us -> 124 us  [local_block(): pl.pallas_call(block_kernel, out_shape=(jax.ShapeDtypeStruct(latents.shap...]
where the time goes in v4:
time: 135 us
  Pallas kernels  124 us (92%)
  other arithmetic  8.67 us (6%)
    pallas_call x1, Pallas kernels, local_block(): pl.pallas_call(block_kernel, out_shape=(jax.ShapeDtypeStruct(latents.shap...  124 us
    broadcast_in_dim x1, other arithmetic, local_block(): return (latent_grad[None], updated[None], first_new[None], second_new[None])  7.37 us

profile of v4, /device:TPU:0, one launch (start us, length us, event | category | flops | bytes accessed | tf_op | source)
XLA Modules:
  0.0 134.5 jit_solution(4953789978699539240)
XLA Ops:
  0.6 1.3 and_reduce_fusion
  1.9 0.0 copy-start
  1.9 0.0 copy-start.1
  1.9 124.1 %shard_map.93 = (bf16[4,16,16,640]{3,2,1,0:T(8,128)(2,1)}, bf16[80,5760]{1,0:T(8,128)(2,1)}, bf16[80,5760]{1,0:T(8,128)(2,1)}, bf16[80,5760]{1,0:T(8,128)(2,1)}, bf16[80,5760]{1,0:T(8,128)(2,1)}) custom-call(s32[4]{0:T(128)} %sources.1, bf16[4,16,16,640]{3,2,1,0:T(8,128)(2,1)} %bitcast.21, f32[80,5760]{1,0:T(8,128)} %bitcast.17, ...), custom_call_target="tpu_custom_call" | custom-call | flops 22649241600 | bytes 16000000 | tf_op jit(solution)/shard_map/pallas_call | solution.py:635
  126.0 0.0 copy-done
  126.1 0.0 copy-done.1
  126.1 0.0 copy-start.2
  126.1 7.4 %fusion.3 = (f32[1,80,5760]{2,1,0:T(8,128)}, f32[1,80,5760]{2,1,0:T(8,128)}, f32[1,80,5760]{2,1,0:T(8,128)}) fusion(bf16[80,5760]{1,0:T(8,128)(2,1)} %get-tuple-element.12, bf16[80,5760]{1,0:T(8,128)(2,1)} %get-tuple-element.13, pred[]{:T(512)} %and_reduce_fusion, f32[1,80,5760]{2,1,0:T(8,128)} %param.10, f32[1,80,5760]{2,1,0:T(8,128)S(1)} %copy-done.1, ...), kind=kLoop, calls=%fused_computation.6 | loop fusion | flops 8755200 | bytes 14745601 | tf_op jit(solution)/shard_map/broadcast_in_dim | solution.py:688
  133.5 0.0 copy-done.2
  133.5 1.1 copy.11
Async XLA Ops:
  1.9 124.1 %copy-start = (f32[1,80,5760]{2,1,0:T(8,128)S(1)}, f32[1,80,5760]{2,1,0:T(8,128)}, u32[]{:S(2)}) copy-start(f32[1,80,5760]{2,1,0:T(8,128)} %param.8) | copy-start | bytes 5529604
  1.9 124.1 %copy-start.1 = (f32[1,80,5760]{2,1,0:T(8,128)S(1)}, f32[1,80,5760]{2,1,0:T(8,128)}, u32[]{:S(2)}) copy-start(f32[1,80,5760]{2,1,0:T(8,128)} %param.9) | copy-start | bytes 5529604
  126.1 7.4 %copy-start.2 = (bf16[4,16,16,640]{3,2,1,0:T(8,128)(2,1)S(1)}, bf16[4,16,16,640]{3,2,1,0:T(8,128)(2,1)}, u32[]{:S(2)}) copy-start(bf16[4,16,16,640]{3,2,1,0:T(8,128)(2,1)} %get-tuple-element.9) | copy-start | bytes 3932164
